TPU v7x, 32 devices: a whole 2x2x4 slice. The times are simulated.
32 devices in a mesh: groups: 2 (over y), shard: 4 (over z), mirror: 4 (over x, core).
Axes of the slice: x: 2, y: 2, z: 4, core: 2. Of those that a mesh axis runs over, the one named last changes fastest.
Arguments:
- embeddings: bfloat16 [16384, 1024], P(('groups', 'shard', 'mirror')), parts along dimension 0, may hold values from -6 to 6
- assignment: int32 [16384], P(('groups', 'shard', 'mirror')), parts along dimension 0, may hold values from 0 to 15, as said below
- counts: int32 [32], P('groups'), parts along dimension 0, may hold values from 64 to 1024, as said below
- slot: int32 [16384], P(('groups', 'shard', 'mirror')), parts along dimension 0, may hold values from 0 to 63, as said below
Outputs:
- dup_score: float32 [16384], P(('groups', 'shard', 'mirror')), parts along dimension 0
- centroids: float32 [32, 1024], P('groups'), parts along dimension 0
There are 2 independent parts, one for each index of `groups`. A program takes and returns all parts, laid end to end along the dimension named above; each array names one. Nothing has to cross between parts.
Inputs may be any that keep to these rules, and one draw needn't show every extreme that they name: `assignment`: among the rows of one device (aligned blocks of 512 rows), at most 64 name one cluster; one cluster is named by exactly 64 rows in every block, and every cluster has exactly 64 rows in some block. `slot`: the rows of one device that name the same cluster have distinct slots. counts[c] is the number of rows of the slab whose assignment is c.
All inputs are finite; a program needn't handle non-finite values.
Results may differ from a plain program's by a relative error of at most 0.0032.
Values may be sent and summed in bfloat16 or wider, within the bound.
A program may use at most 64 MiB of HBM per device.

v0:
```python
import jax
import jax.numpy as jnp
from jax import lax
from jax.sharding import PartitionSpec as P

sharpness = 50.0


def local(embeddings, assignment, counts, slot):
    shard_count = lax.axis_size("shard")
    mirror_count = lax.axis_size("mirror")
    devices_here = shard_count * mirror_count
    rows_here = embeddings.shape[0]
    features = embeddings.shape[1]
    clusters = counts.shape[0]
    capacity = max(2, (2 * rows_here + devices_here - 1) // devices_here)
    width = devices_here * capacity
    wide = embeddings.astype(jnp.float32)
    unit_rows = (wide / jnp.sqrt(jnp.sum(wide * wide, axis=1, keepdims=True) + 1e-06)).astype(
        jnp.bfloat16
    )
    cluster_ids = jnp.arange(clusters, dtype=jnp.int32)
    flat_slot = assignment * capacity + slot
    outgoing = jnp.zeros((width, features), jnp.bfloat16).at[flat_slot].set(unit_rows)
    present = (
        jnp.zeros((width,), jnp.bfloat16).at[flat_slot].set(jnp.ones((rows_here,), jnp.bfloat16))
    )
    outgoing = outgoing.reshape(shard_count, mirror_count, capacity, features)
    present = present.reshape(shard_count, mirror_count, capacity)
    incoming, arrived = (
        lax.all_to_all(
            lax.all_to_all(outgoing, "shard", split_axis=0, concat_axis=0, tiled=True),
            "mirror",
            split_axis=1,
            concat_axis=1,
            tiled=True,
        ),
        lax.all_to_all(
            lax.all_to_all(present, "shard", split_axis=0, concat_axis=0, tiled=True),
            "mirror",
            split_axis=1,
            concat_axis=1,
            tiled=True,
        ),
    )
    members = incoming.reshape(width, features)
    valid = arrived.reshape(width)
    owner = lax.axis_index("shard") * mirror_count + lax.axis_index("mirror")
    count_here = jnp.sum(jnp.where(cluster_ids == owner, counts, 0)).astype(jnp.float32)
    cosine = jnp.dot(members, members.T, preferred_element_type=jnp.float32)
    diagonal = (
        jnp.arange(width, dtype=jnp.int32)[:, None] == jnp.arange(width, dtype=jnp.int32)[None, :]
    )
    weights = jnp.where(
        diagonal, 0.0, jnp.exp(sharpness * cosine) * valid.astype(jnp.float32)[None, :]
    )
    total = jnp.sum(weights, axis=1)
    scores = jnp.log(1.0 + total / count_here).reshape(shard_count, mirror_count, capacity)
    returned = lax.all_to_all(
        lax.all_to_all(scores, "shard", split_axis=0, concat_axis=0, tiled=True),
        "mirror",
        split_axis=1,
        concat_axis=1,
        tiled=True,
    )
    dup_score = returned.reshape(width)[flat_slot]
    onehot_home = (assignment[:, None] == cluster_ids[None, :]).astype(jnp.bfloat16)
    partial_value = jnp.einsum(
        "rk,rd->kd", onehot_home, unit_rows, preferred_element_type=jnp.float32
    )
    own_sum = lax.psum_scatter(partial_value, ("shard", "mirror"), scatter_dimension=0, tiled=True)
    own_centroid = own_sum / jnp.sqrt(jnp.mean(own_sum * own_sum, axis=1, keepdims=True) + 1e-06)
    centroids = lax.all_gather(own_centroid, ("shard", "mirror"), axis=0, tiled=True)
    return (dup_score, centroids)


def solution(mesh):
    placed = (
        P(("groups", "shard", "mirror"), None),
        P(("groups", "shard", "mirror")),
        P("groups"),
        P(("groups", "shard", "mirror")),
    )
    return jax.shard_map(
        local,
        mesh=mesh,
        in_specs=placed,
        out_specs=(P(("groups", "shard", "mirror")), P("groups", None)),
        check_vma=False,
    )
```

profile of v0, /device:TPU:0, one launch (start us, length us, event | category | flops | bytes accessed | tf_op | source)
XLA Modules:
  0.0 231.7 jit_solution(17543580883345804390)
XLA Ops:
  7.2 0.7 compare_select_fusion
  7.9 3.8 %scatter_custom_fusion.1 = bf16[1024]{0:T(1024)(128)(2,1)S(1)} fusion(s32[512]{0:T(512)S(1)} %compare_select_fusion, bf16[512]{0:T(512)(128)(2,1)S(1)} %broadcast.22, bf16[]{:T(256)} %constant.14.clone.1), kind=kCustom, calls=%fused_computation.22 | custom fusion | bytes 2050 | tf_op jit(solution)/shard_map/scatter | solution.py:26
  11.6 0.1 reshape.50
  11.7 0.7 reshape.87
  12.4 6.3 %all-to-all-start.2 = ((bf16[4,2,128]{2,1,0:T(2,128)(2,1)}), bf16[4,2,128]{2,1,0:T(2,128)(2,1)S(1)}, u32[]{:S(2)}, u32[]{:S(2)}) async-start(bf16[4,2,128]{2,1,0:T(2,128)(2,1)} %reshape.87), calls=%async_computation.2 | async-start | bytes 4096 | tf_op jit(solution)/shard_map/all_to_all | solution.py:39
  18.7 1.5 fusion
  20.2 4.9 %scatter_custom_fusion = bf16[1024,1024]{1,0:T(8,128)(2,1)} fusion(s32[512]{0:T(512)S(1)} %compare_select_fusion, bf16[]{:T(256)} %constant.14.clone.1, bf16[512,1024]{1,0:T(8,128)(2,1)} %param.4, f32[512]{0:T(512)S(1)} %add_sqrt_fusion), kind=kCustom, calls=%fused_computation.9 | custom fusion | flops 1572864 | bytes 3147778 | tf_op jit(solution)/shard_map/scatter | solution.py:24
  25.1 0.0 all-to-all-done.2
  25.1 5.1 %all-to-all-start = ((bf16[4,4,64,1024]{3,2,1,0:T(8,128)(2,1)}), bf16[4,4,64,1024]{3,2,1,0:T(8,128)(2,1)S(1)}, u32[]{:S(2)}, u32[]{:S(2)}) async-start(bf16[4,4,64,1024]{3,2,1,0:T(8,128)(2,1)} %bitcast.18), calls=%async_computation | async-start | bytes 4194304 | tf_op jit(solution)/shard_map/all_to_all | solution.py:32
  30.2 0.1 reshape.88
  30.3 0.7 reshape.89
  31.0 46.9 %all-to-all-done = bf16[4,4,64,1024]{3,2,1,0:T(8,128)(2,1)S(1)} async-done(((bf16[4,4,64,1024]{3,2,1,0:T(8,128)(2,1)}), bf16[4,4,64,1024]{3,2,1,0:T(8,128)(2,1)S(1)}, u32[]{:S(2)}, u32[]{:S(2)}) %all-to-all-start) | async-done | bytes 2097184 | tf_op jit(solution)/shard_map/all_to_all | solution.py:32
  77.9 3.2 %all-to-all-start.3 = ((bf16[4,2,128]{2,1,0:T(2,128)(2,1)}), bf16[4,2,128]{2,1,0:T(2,128)(2,1)S(1)}, u32[]{:S(2)}, u32[]{:S(2)}) async-start(bf16[4,2,128]{2,1,0:T(2,128)(2,1)} %reshape.89), calls=%async_computation.3 | async-start | bytes 4096 | tf_op jit(solution)/shard_map/all_to_all | solution.py:38
  81.1 1.6 copy.13
  82.7 0.0 copy-start
  82.7 0.0 copy-start.1
  82.7 2.0 all-to-all-done.3
  84.7 3.6 %all-to-all-start.1 = ((bf16[4,4,64,1024]{3,2,0,1:T(8,128)(2,1)}), bf16[4,4,64,1024]{3,2,0,1:T(8,128)(2,1)S(1)}, u32[]{:S(2)}, u32[]{:S(2)}) async-start(bf16[4,4,64,1024]{3,2,0,1:T(8,128)(2,1)} %copy.13), calls=%async_computation.1 | async-start | bytes 4194304 | tf_op jit(solution)/shard_map/all_to_all | solution.py:31
  88.3 0.0 copy-start.2
  88.4 0.0 copy-start.3
  88.4 0.0 all-reduce.3.cloned.1.call-start
  88.4 0.0 copy-done
  88.4 0.0 copy-done.1
  88.4 1.1 fusion.4
  89.6 0.0 all-reduce.3.cloned.1.call-update
  89.6 0.0 copy-done.2
  89.6 0.6 fusion.8
  90.9 0.0 copy-done.3
  90.9 0.6 dynamic-slice
  91.5 0.1 reshape.90
  91.6 0.1 reshape.52
  91.7 85.8 %all-reduce.3.cloned.1.call-done = f32[16,1024]{1,0:T(8,128)} async-done(((f32[16,1024]{1,0:T(8,128)}), f32[16,1024]{1,0:T(8,128)}) %all-reduce.3.cloned.1.call-update) | async-done | bytes 65552
  177.4 2.0 multiply_reduce_fusion
  180.1 0.0 all-to-all-done.1
  180.2 0.2 copy.14
  180.3 2.6 %select_reduce_fusion = f32[1024]{0:T(1024)S(1)} fusion(bf16[1024,1024]{1,0:T(8,128)(2,1)S(1)} %bitcast.19, f32[1024]{0:T(1024)S(1)} %reshape.52), kind=kOutput, calls=%fused_computation.3 | convolution fusion | flops 2152725504 | bytes 2105344 | tf_op jit(solution)/shard_map/dot_general | solution.py:50
  182.9 0.1 log.8
  183.0 0.7 reshape.91
  183.7 6.2 %all-to-all-start.4 = ((f32[4,1,256]{2,1,0:T(1,128)}), f32[4,1,256]{2,1,0:T(1,128)S(1)}, u32[]{:S(2)}, u32[]{:S(2)}) async-start(f32[4,1,256]{2,1,0:T(1,128)} %reshape.91), calls=%async_computation.4 | async-start | bytes 8192 | tf_op jit(solution)/shard_map/all_to_all | solution.py:60
  189.9 1.4 divide_bitcast_fusion
  191.3 4.2 %all-to-all-done.4 = f32[4,1,256]{2,1,0:T(1,128)S(1)} async-done(((f32[4,1,256]{2,1,0:T(1,128)}), f32[4,1,256]{2,1,0:T(1,128)S(1)}, u32[]{:S(2)}, u32[]{:S(2)}) %all-to-all-start.4) | async-done | bytes 4128 | tf_op jit(solution)/shard_map/all_to_all | solution.py:60
  195.5 0.5 broadcast.30
  196.0 0.7 reduce.1
  196.7 0.1 reshape.92
  196.7 0.7 reshape.93
  197.4 3.2 %all-to-all-start.5 = ((f32[4,1,256]{2,1,0:T(1,128)}), f32[4,1,256]{2,1,0:T(1,128)S(1)}, u32[]{:S(2)}, u32[]{:S(2)}) async-start(f32[4,1,256]{2,1,0:T(1,128)} %reshape.93), calls=%async_computation.5 | async-start | bytes 8192 | tf_op jit(solution)/shard_map/all_to_all | solution.py:59
  200.7 19.2 %all-gather = f32[16,1,1024]{2,1,0:T(1,128)S(1)} all-gather(f32[1,1,1024]{2,1,0:T(1,128)S(1)} %divide_bitcast_fusion), channel_id=1, replica_groups=mesh['groups'=2,'shard'=4,'mirror'=4] {'shard','mirror'}, dimensions={0}, use_global_device_ids=true | all-gather | bytes 69632 | tf_op jit(solution)/shard_map/all_gather | solution.py:73
  219.9 0.6 copy.23
  220.6 0.0 all-to-all-done.5
  220.6 0.7 reduce.2
  221.2 0.1 reshape.94
  221.3 0.1 reshape.51
  221.4 3.4 %gather_fusion = f32[512]{0:T(512)} fusion(f32[1024]{0:T(1024)S(1)} %reshape.51, s32[1024]{0:T(1024)S(1)} %pad_clamp_fusion), kind=kCustom, calls=%fused_computation | custom fusion | bytes 6144 | tf_op jit(solution)/shard_map/gather | solution.py:66
  (8 shorter events, 0.1 us)
Async XLA Ops:
  12.4 12.7 %all-to-all-start.2 = ((bf16[4,2,128]{2,1,0:T(2,128)(2,1)}), bf16[4,2,128]{2,1,0:T(2,128)(2,1)S(1)}, u32[]{:S(2)}, u32[]{:S(2)}) async-start(bf16[4,2,128]{2,1,0:T(2,128)(2,1)} %reshape.87), calls=%async_computation.2 | async-start | bytes 4096 | tf_op jit(solution)/shard_map/all_to_all | solution.py:39
  25.1 52.7 %all-to-all-start = ((bf16[4,4,64,1024]{3,2,1,0:T(8,128)(2,1)}), bf16[4,4,64,1024]{3,2,1,0:T(8,128)(2,1)S(1)}, u32[]{:S(2)}, u32[]{:S(2)}) async-start(bf16[4,4,64,1024]{3,2,1,0:T(8,128)(2,1)} %bitcast.18), calls=%async_computation | async-start | bytes 4194304 | tf_op jit(solution)/shard_map/all_to_all | solution.py:32
  77.9 6.9 %all-to-all-start.3 = ((bf16[4,2,128]{2,1,0:T(2,128)(2,1)}), bf16[4,2,128]{2,1,0:T(2,128)(2,1)S(1)}, u32[]{:S(2)}, u32[]{:S(2)}) async-start(bf16[4,2,128]{2,1,0:T(2,128)(2,1)} %reshape.89), calls=%async_computation.3 | async-start | bytes 4096 | tf_op jit(solution)/shard_map/all_to_all | solution.py:38
  82.7 5.7 %copy-start = (bf16[512,1024]{1,0:T(8,128)(2,1)S(1)}, bf16[512,1024]{1,0:T(8,128)(2,1)}, u32[]{:S(2)}) copy-start(bf16[512,1024]{1,0:T(8,128)(2,1)} %param.4) | copy-start | bytes 3145732
  82.7 5.7 %copy-start.1 = (s32[512]{0:T(512)S(1)}, s32[512]{0:T(512)}, u32[]{:S(2)}) copy-start(s32[512]{0:T(512)} %param.5) | copy-start | bytes 6148
  84.7 95.4 %all-to-all-start.1 = ((bf16[4,4,64,1024]{3,2,0,1:T(8,128)(2,1)}), bf16[4,4,64,1024]{3,2,0,1:T(8,128)(2,1)S(1)}, u32[]{:S(2)}, u32[]{:S(2)}) async-start(bf16[4,4,64,1024]{3,2,0,1:T(8,128)(2,1)} %copy.13), calls=%async_computation.1 | async-start | bytes 4194304 | tf_op jit(solution)/shard_map/all_to_all | solution.py:31
  88.3 1.3 copy-start.2
  88.4 2.6 %copy-start.3 = (u32[32]{0:T(128)S(1)}, u32[32]{0:T(128)}, u32[]{:S(2)}) copy-start(u32[32]{0:T(128)} %constant.37) | copy-start | bytes 388
  88.4 89.1 %all-reduce.3.cloned.1.call-start = ((), (), s32[]{:S(2)}) async-start(), calls=%async_computation.6 | async-start | bytes 131072
  183.7 11.8 %all-to-all-start.4 = ((f32[4,1,256]{2,1,0:T(1,128)}), f32[4,1,256]{2,1,0:T(1,128)S(1)}, u32[]{:S(2)}, u32[]{:S(2)}) async-start(f32[4,1,256]{2,1,0:T(1,128)} %reshape.91), calls=%async_computation.4 | async-start | bytes 8192 | tf_op jit(solution)/shard_map/all_to_all | solution.py:60
  197.4 23.1 %all-to-all-start.5 = ((f32[4,1,256]{2,1,0:T(1,128)}), f32[4,1,256]{2,1,0:T(1,128)S(1)}, u32[]{:S(2)}, u32[]{:S(2)}) async-start(f32[4,1,256]{2,1,0:T(1,128)} %reshape.93), calls=%async_computation.5 | async-start | bytes 8192 | tf_op jit(solution)/shard_map/all_to_all | solution.py:59
Sparse Core Ops, SparseCore 0:
  93.2 84.1 all-reduce.2
where the time goes:
time: 232 us
  waiting for transfers between devices  139 us (60%)
  starting transfers between devices  27.7 us (12%)
  blocking collectives  19.2 us (8%)
  between operations  15.5 us (7%)
  local copies, waits for them, and re-layouts  14.1 us (6%)
  other arithmetic  12.5 us (5%)
  matrix products  3.73 us (2%)
    unnamed x2, waiting for transfers between devices  85.8 us
    all_to_all x1, waiting for transfers between devices, local(): lax.all_to_all(outgoing, 'shard', split_axis=0, concat_axis=0, tiled=True)  46.9 us
    all_gather x1, blocking collectives, local(): lax.all_gather(own_centroid, ('shard', 'mirror'), axis=0, tiled=True)  19.2 us
    all_to_all x1, starting transfers between devices, local(): lax.all_to_all(present, 'shard', split_axis=0, concat_axis=0, tiled=True)  6.32 us
    all_to_all x1, starting transfers between devices, local(): lax.all_to_all(scores, 'shard', split_axis=0, concat_axis=0, tiled=True)  6.19 us
    all_to_all x1, starting transfers between devices, local(): lax.all_to_all(outgoing, 'shard', split_axis=0, concat_axis=0, tiled=True)  5.09 us
    scatter x1, other arithmetic, local(): jnp.zeros((width, features), jnp.bfloat16).at[flat_slot].set(unit_rows)  4.91 us
  transfers between devices with their start and end apart: 7, of which 4 were waited for; matrix products, arithmetic and copies ran while one was open for 7% of the time, Pallas kernels for 0%

commit v1 on v0

v1 whole, which is shorter than its diff:
```python
import functools

import jax
import jax.numpy as jnp
from jax import lax
from jax.experimental import pallas as pl
from jax.experimental.pallas import tpu as pltpu
from jax.sharding import PartitionSpec as P

sharpness = 50.0
f32, bf16 = jnp.float32, jnp.bfloat16


def flipped(index, mask):
    result, place = index, 1
    while place <= mask:
        if mask & place:
            bit = lax.rem(lax.div(index, place), 2)
            result = result + place * (1 - 2 * bit)
        place *= 2
    return result


def visiting_order(shards, mirrors):
    masks = [dz * mirrors + dm for dz in range(shards) for dm in range(mirrors)]
    far = lambda mask: (-(mask // mirrors), mask % mirrors)
    return [0] + sorted([m for m in masks if m], key=far)


def kernel(
    shards,
    mirrors,
    emb_ref,
    assign_ref,
    slot_ref,
    counts_ref,
    score_ref,
    cent_ref,
    place,
    outgoing,
    members,
    total,
    score_out,
    score_in,
    cent_all,
    row_send,
    row_recv,
    score_send,
    score_recv,
    cent_send,
    cent_recv,
):
    n = shards * mirrors
    rows, features = emb_ref.shape
    width = members.shape[0]
    cap = width // n
    pair = 2 * cap
    order = visiting_order(shards, mirrors)
    my_shard, my_mirror = lax.axis_index("shard"), lax.axis_index("mirror")
    me = my_shard * mirrors + my_mirror

    def peer(q):
        return {
            "shard": flipped(my_shard, order[q] // mirrors),
            "mirror": flipped(my_mirror, order[q] % mirrors),
        }

    def remote(src, dst, send, recv, q):
        return pltpu.make_async_remote_copy(
            src_ref=src,
            dst_ref=dst,
            send_sem=send.at[q],
            recv_sem=recv.at[q],
            device_id=peer(q),
            device_id_type=pl.DeviceIdType.MESH,
        )

    barrier = pltpu.get_barrier_semaphore()
    for q in range(1, n):
        pl.semaphore_signal(
            barrier, inc=1, device_id=peer(q), device_id_type=pl.DeviceIdType.MESH
        )

    wide = emb_ref[...].astype(f32)
    square = jnp.sum(wide * wide, axis=1, keepdims=True) + 1e-06
    unit_rows = (wide * (1.0 / jnp.sqrt(square))).astype(bf16)
    mask_of = assign_ref[...] ^ me
    position = jnp.zeros_like(mask_of)
    for q in range(n):
        position = jnp.where(mask_of == order[q], q, position)
    flat_slot = position * cap + slot_ref[...]

    row_copies = {
        q: remote(
            outgoing.at[pl.ds(q * cap, cap)],
            members.at[pl.ds(q * cap, cap)],
            row_send,
            row_recv,
            q,
        )
        for q in range(1, n)
    }
    batch = 4
    for first in range(0, n, batch):
        span = batch * cap
        slots = lax.broadcasted_iota(jnp.int32, (span, rows), 0) + first * cap
        hot = jnp.where(slots == flat_slot, 1.0, 0.0).astype(bf16)
        place[pl.ds(first * cap, span), :] = hot
        block = jnp.dot(hot, unit_rows, preferred_element_type=f32).astype(bf16)
        if first == 0:
            members[pl.ds(0, cap), :] = block[:cap]
            outgoing[pl.ds(cap, span - cap), :] = block[cap:]
            pl.semaphore_wait(barrier, n - 1)
        else:
            outgoing[pl.ds(first * cap, span), :] = block
        for q in range(max(first, 1), first + batch):
            row_copies[q].start()

    count = jnp.sum(
        jnp.where(
            lax.broadcasted_iota(jnp.int32, counts_ref.shape, 1) == me, counts_ref[...], 0
        ),
        axis=1,
        keepdims=True,
    ).astype(f32)

    def cosine(a, b):
        return lax.dot_general(a, b, (((1,), (1,)), ((), ())), preferred_element_type=f32)

    def fold(x):
        return jnp.sum(x.reshape(x.shape[0] // 8, 8, x.shape[1]), axis=0)

    own = lax.broadcasted_iota(jnp.int32, (pair, pair), 0) == lax.broadcasted_iota(
        jnp.int32, (pair, pair), 1
    )
    sums = jnp.zeros((8, features), f32)
    for p in range(n // 2):
        for q in (2 * p, 2 * p + 1):
            if q > 0:
                row_copies[q].wait_recv()
        fresh = members[pl.ds(p * pair, pair), :]
        sums = sums + fold(fresh.astype(f32))
        within = jnp.where(own, 0.0, jnp.exp(sharpness * cosine(fresh, fresh)) - 1.0)
        gained = fold(within)
        if p > 0:
            old = members[pl.ds(0, p * pair), :]
            gained = gained + fold(jnp.exp(sharpness * cosine(old, fresh)) - 1.0)
            total[:, pl.ds(0, p * pair)] += fold(jnp.exp(sharpness * cosine(fresh, old)) - 1.0)
        total[:, pl.ds(p * pair, pair)] = gained

    sum_row = jnp.sum(sums, axis=0, keepdims=True)
    cent_all[me] = sum_row / jnp.sqrt(jnp.mean(sum_row * sum_row, axis=1, keepdims=True) + 1e-06)
    cent_copies = {
        q: remote(cent_all.at[me], cent_all.at[me], cent_send, cent_recv, q) for q in range(1, n)
    }
    for q in range(1, n):
        cent_copies[q].start()

    sum_here = jnp.sum(total[...], axis=0, keepdims=True) + (count - 1.0)
    scores = jnp.log(1.0 + sum_here / count)
    for p in range(n // 2):
        score_out[p] = scores[:, p * pair : (p + 1) * pair]
    score_copies = {
        q: remote(score_out.at[q // 2], score_in.at[q], score_send, score_recv, q)
        for q in range(1, n)
    }
    for q in range(1, n):
        score_copies[q].start()

    score_in[0] = score_out[0]
    for q in range(1, n):
        score_copies[q].wait_recv()
    low = lax.broadcasted_iota(jnp.int32, (1, pair), 1) < cap
    returned = jnp.concatenate(
        [jnp.where(low, score_in[2 * p], score_in[2 * p + 1]) for p in range(n // 2)], axis=1
    )
    high = returned.astype(bf16)
    rest = returned - high.astype(f32)
    middle = rest.astype(bf16)
    little = (rest - middle.astype(f32)).astype(bf16)
    terms = jnp.concatenate(
        [high, middle, little, jnp.zeros((13, width), bf16)], axis=0
    )
    picked = jnp.dot(terms, place[...], preferred_element_type=f32)
    score_ref[...] = picked[0:1] + (picked[1:2] + picked[2:3])

    for q in range(1, n):
        cent_copies[q].wait_recv()
    for c in range(n):
        cent_ref[pl.ds(c, 1), :] = cent_all[c]
    for q in range(1, n):
        row_copies[q].wait_send()
        score_copies[q].wait_send()
        cent_copies[q].wait_send()


def fused(embeddings, assignment, counts, slot, capacity):
    shards, mirrors = lax.axis_size("shard"), lax.axis_size("mirror")
    n = shards * mirrors
    rows, features = embeddings.shape
    width = n * capacity
    vmem = pl.BlockSpec(memory_space=pltpu.VMEM)
    sems = [pltpu.SemaphoreType.DMA((n,))] * 6
    scores, centroids = pl.pallas_call(
        functools.partial(kernel, shards, mirrors),
        out_shape=(
            jax.ShapeDtypeStruct((1, rows), f32),
            jax.ShapeDtypeStruct((n, features), f32),
        ),
        in_specs=[vmem] * 4,
        out_specs=(vmem, vmem),
        scratch_shapes=[
            pltpu.VMEM((width, rows), bf16),
            pltpu.VMEM((width, features), bf16),
            pltpu.VMEM((width, features), bf16),
            pltpu.VMEM((8, width), f32),
            pltpu.VMEM((n // 2, 1, 2 * capacity), f32),
            pltpu.VMEM((n, 1, 2 * capacity), f32),
            pltpu.VMEM((n, 1, features), f32),
        ]
        + sems,
        compiler_params=pltpu.CompilerParams(
            collective_id=0, has_side_effects=True, vmem_limit_bytes=40 * 2**20
        ),
    )(embeddings, assignment[None, :], slot[None, :], counts[None, :])
    return scores.reshape(rows), centroids


def general(embeddings, assignment, counts, slot, capacity):
    shard_count = lax.axis_size("shard")
    mirror_count = lax.axis_size("mirror")
    rows_here, features = embeddings.shape
    clusters = counts.shape[0]
    width = shard_count * mirror_count * capacity

    def exchange(x):
        x = lax.all_to_all(x, "shard", split_axis=0, concat_axis=0, tiled=True)
        return lax.all_to_all(x, "mirror", split_axis=1, concat_axis=1, tiled=True)

    wide = embeddings.astype(f32)
    unit_rows = (wide / jnp.sqrt(jnp.sum(wide * wide, axis=1, keepdims=True) + 1e-06)).astype(bf16)
    cluster_ids = jnp.arange(clusters, dtype=jnp.int32)
    flat_slot = assignment * capacity + slot
    outgoing = jnp.zeros((width, features), bf16).at[flat_slot].set(unit_rows)
    present = jnp.zeros((width,), bf16).at[flat_slot].set(jnp.ones((rows_here,), bf16))
    members = exchange(outgoing.reshape(shard_count, mirror_count, capacity, features)).reshape(
        width, features
    )
    valid = exchange(present.reshape(shard_count, mirror_count, capacity)).reshape(width)
    owner = lax.axis_index("shard") * mirror_count + lax.axis_index("mirror")
    count_here = jnp.sum(jnp.where(cluster_ids == owner, counts, 0)).astype(f32)
    cosine = jnp.dot(members, members.T, preferred_element_type=f32)
    index = jnp.arange(width, dtype=jnp.int32)
    weights = jnp.where(
        index[:, None] == index[None, :],
        0.0,
        jnp.exp(sharpness * cosine) * valid.astype(f32)[None, :],
    )
    total = jnp.sum(weights, axis=1)
    scores = jnp.log(1.0 + total / count_here).reshape(shard_count, mirror_count, capacity)
    dup_score = exchange(scores).reshape(width)[flat_slot]
    onehot_home = (assignment[:, None] == cluster_ids[None, :]).astype(bf16)
    partial_value = jnp.einsum("rk,rd->kd", onehot_home, unit_rows, preferred_element_type=f32)
    own_sum = lax.psum_scatter(partial_value, ("shard", "mirror"), scatter_dimension=0, tiled=True)
    own_centroid = own_sum / jnp.sqrt(jnp.mean(own_sum * own_sum, axis=1, keepdims=True) + 1e-06)
    centroids = lax.all_gather(own_centroid, ("shard", "mirror"), axis=0, tiled=True)
    return (dup_score, centroids)


def local(embeddings, assignment, counts, slot):
    devices_here = lax.axis_size("shard") * lax.axis_size("mirror")
    capacity = max(2, (2 * embeddings.shape[0] + devices_here - 1) // devices_here)
    powers = devices_here & (devices_here - 1) == 0 and devices_here % 4 == 0
    whole_tiles = capacity % 16 == 0 and (2 * capacity) % 128 == 0
    form = fused if powers and whole_tiles and counts.shape[0] == devices_here else general
    return form(embeddings, assignment, counts, slot, capacity)


def solution(mesh):
    placed = (
        P(("groups", "shard", "mirror"), None),
        P(("groups", "shard", "mirror")),
        P("groups"),
        P(("groups", "shard", "mirror")),
    )
    return jax.shard_map(
        local,
        mesh=mesh,
        in_specs=placed,
        out_specs=(P(("groups", "shard", "mirror")), P("groups", None)),
        check_vma=False,
    )
```

time: 232 us -> 71 us (0.31)
  waiting for transfers between devices: 139 us -> 0 us
  Pallas kernels: 0 us -> 67.1 us
  starting transfers between devices: 27.7 us -> 0 us
  blocking collectives: 19.2 us -> 0 us
  between operations: 15.5 us -> 0.67 us
  other arithmetic: 12.5 us -> 0 us
  local copies, waits for them, and re-layouts: 14.1 us -> 3.11 us
  matrix products: 3.73 us -> 0 us
    unnamed x2 -> x0, waiting for transfers between devices: 85.8 us -> none
    pallas_call x0 -> x1, Pallas kernels: none -> 67.1 us  [fused(): pl.pallas_call(functools.partial(kernel, shards, mirrors), out_shape=(jax...]
    all_to_all x6 -> x0, waiting for transfers between devices: 53.1 us -> none  [the longest x1 46.9 us: local(): lax.all_to_all(outgoing, 'shard', split_axis=0, concat_axis=0, tiled=True)]
    all_to_all x6 -> x0, starting transfers between devices: 27.7 us -> none  [the longest x1 6.32 us: local(): lax.all_to_all(present, 'shard', split_axis=0, concat_axis=0, tiled=True)]
    all_gather x1 -> x0, blocking collectives: 19.2 us -> none  [local(): lax.all_gather(own_centroid, ('shard', 'mirror'), axis=0, tiled=True)]
    scatter x1 -> x0, other arithmetic: 4.91 us -> none  [local(): jnp.zeros((width, features), jnp.bfloat16).at[flat_slot].set(unit_rows)]
    reduce_sum x3 -> x0, other arithmetic: 4.15 us -> none  [the longest x1 2.02 us: local(): jnp.mean(own_sum * own_sum, axis=1, keepdims=True) + 1e-06]
    scatter x1 -> x0, local copies, waits for them, and re-layouts: 3.77 us -> none  [local(): jnp.zeros((width,), jnp.bfloat16).at[flat_slot]]
  transfers between devices with their start and end apart: 7 -> 0, of which waited for: 4 -> 0; matrix products, arithmetic and copies ran while one was open for 7% -> 0% of each run, Pallas kernels for 0% -> 0%
where the time goes in v1:
time: 71 us; the launch traced here: 70.9 us
  Pallas kernels  67.1 us (95%)
  local copies, waits for them, and re-layouts  3.11 us (4%)
    pallas_call x1, Pallas kernels, fused(): pl.pallas_call(functools.partial(kernel, shards, mirrors), out_shape=(jax...  67.1 us
    unnamed x10, local copies, waits for them, and re-layouts  3.11 us

profile of v1, /device:TPU:0, one launch (start us, length us, event | category | flops | bytes accessed | tf_op | source)
XLA Modules:
  0.0 70.9 jit_solution(13242112599081373551)
XLA Ops:
  0.6 0.0 copy-start.2
  0.6 0.0 copy-start.1
  0.7 0.0 copy-start.3
  0.7 0.7 copy-done.2
  1.3 0.0 copy-done.1
  1.3 0.0 copy-done.3
  1.3 0.0 copy-start
  1.3 1.2 %copy-done = bf16[512,1024]{1,0:T(8,128)(2,1)S(1)} copy-done((bf16[512,1024]{1,0:T(8,128)(2,1)S(1)}, bf16[512,1024]{1,0:T(8,128)(2,1)}, u32[]{:S(2)}) %copy-start) | copy-done | bytes 1048600
  2.6 67.1 %shard_map.59 = (f32[1,512]{1,0:T(1,128)S(1)}, f32[16,1024]{1,0:T(8,128)S(1)}) custom-call(bf16[512,1024]{1,0:T(8,128)(2,1)S(1)} %copy-done, s32[1,512]{1,0:T(1,128)S(1)} %bitcast.4, s32[1,512]{1,0:T(1,128)S(1)} %bitcast.5, s32[1,16]{1,0:T(1,128)S(1)} %bitcast.7), custom_call_target="tpu_custom_call" | custom-call | tf_op jit(solution)/shard_map/pallas_call | solution.py:204
  69.6 0.6 copy.8
  70.2 0.6 copy.9
Async XLA Ops:
  0.6 0.7 copy-start.2
  0.6 0.7 copy-start.1
  0.7 0.7 copy-start.3
  1.3 1.2 %copy-start = (bf16[512,1024]{1,0:T(8,128)(2,1)S(1)}, bf16[512,1024]{1,0:T(8,128)(2,1)}, u32[]{:S(2)}) copy-start(bf16[512,1024]{1,0:T(8,128)(2,1)} %emb_ref.1) | copy-start | bytes 3145732

commit v2 on v1

--- a/solution.py
+++ b/solution.py
@@ -21,48 +21,45 @@
     return result
 
 
-def visiting_order(shards, mirrors):
-    masks = [dz * mirrors + dm for dz in range(shards) for dm in range(mirrors)]
-    far = lambda mask: (-(mask // mirrors), mask % mirrors)
-    return [0] + sorted([m for m in masks if m], key=far)
-
-
 def kernel(
     shards,
     mirrors,
-    emb_ref,
-    assign_ref,
-    slot_ref,
-    counts_ref,
+    sends,
+    emb_hbm,
+    assign_hbm,
+    slot_hbm,
+    counts_hbm,
     score_ref,
     cent_ref,
+    emb,
+    assign,
+    slot,
+    counts,
     place,
     outgoing,
     members,
-    total,
-    score_out,
-    score_in,
-    cent_all,
+    across,
+    down,
+    reply_out,
+    reply_in,
+    load_sem,
     row_send,
     row_recv,
-    score_send,
-    score_recv,
-    cent_send,
-    cent_recv,
+    reply_send,
+    reply_recv,
 ):
     n = shards * mirrors
-    rows, features = emb_ref.shape
+    rows, features = emb.shape
     width = members.shape[0]
     cap = width // n
     pair = 2 * cap
-    order = visiting_order(shards, mirrors)
     my_shard, my_mirror = lax.axis_index("shard"), lax.axis_index("mirror")
     me = my_shard * mirrors + my_mirror
 
     def peer(q):
         return {
-            "shard": flipped(my_shard, order[q] // mirrors),
-            "mirror": flipped(my_mirror, order[q] % mirrors),
+            "shard": flipped(my_shard, q // mirrors),
+            "mirror": flipped(my_mirror, q % mirrors),
         }
 
     def remote(src, dst, send, recv, q):
@@ -75,21 +72,23 @@
             device_id_type=pl.DeviceIdType.MESH,
         )
 
+    loads = [
+        pltpu.make_async_copy(src, dst, load_sem.at[k])
+        for k, (src, dst) in enumerate(
+            [(assign_hbm, assign), (slot_hbm, slot), (emb_hbm, emb), (counts_hbm, counts)]
+        )
+    ]
+    for load in loads:
+        load.start()
     barrier = pltpu.get_barrier_semaphore()
     for q in range(1, n):
         pl.semaphore_signal(
             barrier, inc=1, device_id=peer(q), device_id_type=pl.DeviceIdType.MESH
         )
-
-    wide = emb_ref[...].astype(f32)
-    square = jnp.sum(wide * wide, axis=1, keepdims=True) + 1e-06
-    unit_rows = (wide * (1.0 / jnp.sqrt(square))).astype(bf16)
-    mask_of = assign_ref[...] ^ me
-    position = jnp.zeros_like(mask_of)
-    for q in range(n):
-        position = jnp.where(mask_of == order[q], q, position)
-    flat_slot = position * cap + slot_ref[...]
-
+    for load in loads:
+        load.wait()
+
+    flat_slot = (assign[...] ^ me) * cap + slot[...]
     row_copies = {
         q: remote(
             outgoing.at[pl.ds(q * cap, cap)],
@@ -100,32 +99,28 @@
         )
         for q in range(1, n)
     }
-    batch = 4
-    for first in range(0, n, batch):
-        span = batch * cap
+    span = mirrors * cap
+    for turn, dz in enumerate(sends):
+        first = dz * mirrors
         slots = lax.broadcasted_iota(jnp.int32, (span, rows), 0) + first * cap
         hot = jnp.where(slots == flat_slot, 1.0, 0.0).astype(bf16)
         place[pl.ds(first * cap, span), :] = hot
-        block = jnp.dot(hot, unit_rows, preferred_element_type=f32).astype(bf16)
+        block = jnp.dot(hot, emb[...], preferred_element_type=f32).astype(bf16)
         if first == 0:
             members[pl.ds(0, cap), :] = block[:cap]
             outgoing[pl.ds(cap, span - cap), :] = block[cap:]
-            pl.semaphore_wait(barrier, n - 1)
         else:
             outgoing[pl.ds(first * cap, span), :] = block
-        for q in range(max(first, 1), first + batch):
+        if turn == 0:
+            pl.semaphore_wait(barrier, n - 1)
+        for q in range(max(first, 1), first + mirrors):
             row_copies[q].start()
 
     count = jnp.sum(
-        jnp.where(
-            lax.broadcasted_iota(jnp.int32, counts_ref.shape, 1) == me, counts_ref[...], 0
-        ),
+        jnp.where(lax.broadcasted_iota(jnp.int32, counts.shape, 1) == me, counts[...], 0),
         axis=1,
         keepdims=True,
     ).astype(f32)
-
-    def cosine(a, b):
-        return lax.dot_general(a, b, (((1,), (1,)), ((), ())), preferred_element_type=f32)
 
     def fold(x):
         return jnp.sum(x.reshape(x.shape[0] // 8, 8, x.shape[1]), axis=0)
@@ -138,60 +133,76 @@
         for q in (2 * p, 2 * p + 1):
             if q > 0:
                 row_copies[q].wait_recv()
-        fresh = members[pl.ds(p * pair, pair), :]
+        wide = members[pl.ds(p * pair, pair), :].astype(f32)
+        square = jnp.sum(wide * wide, axis=1, keepdims=True) + 1e-06
+        fresh = (wide * (1.0 / jnp.sqrt(square))).astype(bf16)
+        members[pl.ds(p * pair, pair), :] = fresh
         sums = sums + fold(fresh.astype(f32))
-        within = jnp.where(own, 0.0, jnp.exp(sharpness * cosine(fresh, fresh)) - 1.0)
-        gained = fold(within)
+        cosine = lax.dot_general(
+            members[pl.ds(0, (p + 1) * pair), :],
+            fresh,
+            (((1,), (1,)), ((), ())),
+            preferred_element_type=f32,
+        )
+        grown = jnp.exp(sharpness * cosine) - 1.0
+        within = jnp.where(own, 0.0, grown[p * pair :])
         if p > 0:
-            old = members[pl.ds(0, p * pair), :]
-            gained = gained + fold(jnp.exp(sharpness * cosine(old, fresh)) - 1.0)
-            total[:, pl.ds(0, p * pair)] += fold(jnp.exp(sharpness * cosine(fresh, old)) - 1.0)
-        total[:, pl.ds(p * pair, pair)] = gained
+            across[pl.ds(0, p * pair), :] += grown[: p * pair]
+            within_and_old = fold(within) + fold(grown[: p * pair])
+        else:
+            within_and_old = fold(within)
+        across[pl.ds(p * pair, pair), :] = jnp.zeros((pair, pair), f32)
+        down[:, pl.ds(p * pair, pair)] = within_and_old
 
     sum_row = jnp.sum(sums, axis=0, keepdims=True)
-    cent_all[me] = sum_row / jnp.sqrt(jnp.mean(sum_row * sum_row, axis=1, keepdims=True) + 1e-06)
-    cent_copies = {
-        q: remote(cent_all.at[me], cent_all.at[me], cent_send, cent_recv, q) for q in range(1, n)
-    }
-    for q in range(1, n):
-        cent_copies[q].start()
-
-    sum_here = jnp.sum(total[...], axis=0, keepdims=True) + (count - 1.0)
+    centroid = sum_row / jnp.sqrt(jnp.mean(sum_row * sum_row, axis=1, keepdims=True) + 1e-06)
+
+    lanes = across[...]
+    high = lanes.astype(bf16)
+    low = (lanes - high.astype(f32)).astype(bf16)
+    ones = jnp.ones((16, 2 * pair), bf16)
+    turned = lax.dot_general(
+        ones,
+        jnp.concatenate([high, low], axis=1),
+        (((1,), (1,)), ((), ())),
+        preferred_element_type=f32,
+    )
+    sum_here = jnp.sum(down[...], axis=0, keepdims=True) + turned[0:1] + (count - 1.0)
     scores = jnp.log(1.0 + sum_here / count)
     for p in range(n // 2):
-        score_out[p] = scores[:, p * pair : (p + 1) * pair]
-    score_copies = {
-        q: remote(score_out.at[q // 2], score_in.at[q], score_send, score_recv, q)
+        reply_out[p] = jnp.concatenate([centroid, scores[:, p * pair : (p + 1) * pair]], axis=1)
+    reply_copies = {
+        q: remote(reply_out.at[q // 2], reply_in.at[q], reply_send, reply_recv, q)
         for q in range(1, n)
     }
+    for q in range(n - 1, 0, -1):
+        reply_copies[q].start()
+    reply_in[0] = reply_out[0]
     for q in range(1, n):
-        score_copies[q].start()
-
-    score_in[0] = score_out[0]
+        row_copies[q].wait_send()
     for q in range(1, n):
-        score_copies[q].wait_recv()
-    low = lax.broadcasted_iota(jnp.int32, (1, pair), 1) < cap
+        reply_copies[q].wait_recv()
+    first_half = lax.broadcasted_iota(jnp.int32, (1, pair), 1) < cap
     returned = jnp.concatenate(
-        [jnp.where(low, score_in[2 * p], score_in[2 * p + 1]) for p in range(n // 2)], axis=1
+        [
+            jnp.where(first_half, reply_in[2 * p, :, features:], reply_in[2 * p + 1, :, features:])
+            for p in range(n // 2)
+        ],
+        axis=1,
     )
     high = returned.astype(bf16)
     rest = returned - high.astype(f32)
     middle = rest.astype(bf16)
     little = (rest - middle.astype(f32)).astype(bf16)
-    terms = jnp.concatenate(
-        [high, middle, little, jnp.zeros((13, width), bf16)], axis=0
-    )
+    terms = jnp.concatenate([high, middle, little, jnp.zeros((13, width), bf16)], axis=0)
     picked = jnp.dot(terms, place[...], preferred_element_type=f32)
     score_ref[...] = picked[0:1] + (picked[1:2] + picked[2:3])
-
+    for q in range(n):
+        there = peer(q)
+        cluster = there["shard"] * mirrors + there["mirror"]
+        cent_ref[pl.ds(cluster, 1), :] = reply_in[q, :, :features]
     for q in range(1, n):
-        cent_copies[q].wait_recv()
-    for c in range(n):
-        cent_ref[pl.ds(c, 1), :] = cent_all[c]
-    for q in range(1, n):
-        row_copies[q].wait_send()
-        score_copies[q].wait_send()
-        cent_copies[q].wait_send()
+        reply_copies[q].wait_send()
 
 
 def fused(embeddings, assignment, counts, slot, capacity):
@@ -199,26 +210,34 @@
     n = shards * mirrors
     rows, features = embeddings.shape
     width = n * capacity
+    pair = 2 * capacity
     vmem = pl.BlockSpec(memory_space=pltpu.VMEM)
-    sems = [pltpu.SemaphoreType.DMA((n,))] * 6
+    anywhere = pl.BlockSpec(memory_space=pl.ANY)
+    half = max(1, shards // 2)
+    sends = sorted(range(shards), key=lambda dz: (dz % half, -dz))
     scores, centroids = pl.pallas_call(
-        functools.partial(kernel, shards, mirrors),
+        functools.partial(kernel, shards, mirrors, sends),
         out_shape=(
             jax.ShapeDtypeStruct((1, rows), f32),
             jax.ShapeDtypeStruct((n, features), f32),
         ),
-        in_specs=[vmem] * 4,
+        in_specs=[anywhere] * 4,
         out_specs=(vmem, vmem),
         scratch_shapes=[
+            pltpu.VMEM((rows, features), bf16),
+            pltpu.VMEM((1, rows), jnp.int32),
+            pltpu.VMEM((1, rows), jnp.int32),
+            pltpu.VMEM((1, n), jnp.int32),
             pltpu.VMEM((width, rows), bf16),
             pltpu.VMEM((width, features), bf16),
             pltpu.VMEM((width, features), bf16),
+            pltpu.VMEM((width, pair), f32),
             pltpu.VMEM((8, width), f32),
-            pltpu.VMEM((n // 2, 1, 2 * capacity), f32),
-            pltpu.VMEM((n, 1, 2 * capacity), f32),
-            pltpu.VMEM((n, 1, features), f32),
+            pltpu.VMEM((n // 2, 1, features + pair), f32),
+            pltpu.VMEM((n, 1, features + pair), f32),
+            pltpu.SemaphoreType.DMA((4,)),
         ]
-        + sems,
+        + [pltpu.SemaphoreType.DMA((n,))] * 4,
         compiler_params=pltpu.CompilerParams(
             collective_id=0, has_side_effects=True, vmem_limit_bytes=40 * 2**20
         ),

time: 71 us -> 63.8 us (0.90)
  Pallas kernels: 67.1 us -> 59.8 us
    pallas_call x1, Pallas kernels: 67.1 us -> 59.8 us  [fused(): pl.pallas_call(functools.partial(kernel, shards, mirrors, sends), out_sha...]
where the time goes in v2:
time: 63.8 us; the launch traced here: 63.6 us
  Pallas kernels  59.8 us (94%)
  local copies, waits for them, and re-layouts  3.11 us (5%)
  between operations  0.67 us (1%)
    pallas_call x1, Pallas kernels, fused(): pl.pallas_call(functools.partial(kernel, shards, mirrors, sends), out_sha...  59.8 us
    unnamed x10, local copies, waits for them, and re-layouts  3.11 us

profile of v2, /device:TPU:0, one launch (start us, length us, event | category | flops | bytes accessed | tf_op | source)
XLA Modules:
  0.0 63.6 jit_solution(7710828686733918317)
XLA Ops:
  0.6 0.0 copy-start.2
  0.6 0.0 copy-start.1
  0.7 0.0 copy-start.3
  0.7 0.7 %copy-done.2 = s32[512]{0:T(512)S(1)} copy-done((s32[512]{0:T(512)S(1)}, s32[512]{0:T(512)}, u32[]{:S(2)}) %copy-start.2) | copy-done | bytes 2072
  1.3 0.0 copy-done.1
  1.3 0.0 copy-done.3
  1.3 0.0 copy-start
  1.3 1.2 %copy-done = bf16[512,1024]{1,0:T(8,128)(2,1)S(1)} copy-done((bf16[512,1024]{1,0:T(8,128)(2,1)S(1)}, bf16[512,1024]{1,0:T(8,128)(2,1)}, u32[]{:S(2)}) %copy-start) | copy-done | bytes 1048600
  2.6 59.8 %shard_map.59 = (f32[1,512]{1,0:T(1,128)S(1)}, f32[16,1024]{1,0:T(8,128)S(1)}) custom-call(bf16[512,1024]{1,0:T(8,128)(2,1)S(1)} %copy-done, s32[1,512]{1,0:T(1,128)S(1)} %bitcast.4, s32[1,512]{1,0:T(1,128)S(1)} %bitcast.5, s32[1,16]{1,0:T(1,128)S(1)} %bitcast.7), custom_call_target="tpu_custom_call" | custom-call | tf_op jit(solution)/shard_map/pallas_call | solution.py:218
  62.4 0.6 copy.8
  63.0 0.6 copy.9
Async XLA Ops:
  0.6 0.7 %copy-start.2 = (s32[512]{0:T(512)S(1)}, s32[512]{0:T(512)}, u32[]{:S(2)}) copy-start(s32[512]{0:T(512)} %param.7) | copy-start | bytes 6148
  0.6 0.7 %copy-start.1 = (s32[512]{0:T(512)S(1)}, s32[512]{0:T(512)}, u32[]{:S(2)}) copy-start(s32[512]{0:T(512)} %param.5) | copy-start | bytes 6148
  0.7 0.7 %copy-start.3 = (s32[16]{0:T(128)S(1)}, s32[16]{0:T(128)}, u32[]{:S(2)}) copy-start(s32[16]{0:T(128)} %param.6) | copy-start | bytes 196
  1.3 1.2 %copy-start = (bf16[512,1024]{1,0:T(8,128)(2,1)S(1)}, bf16[512,1024]{1,0:T(8,128)(2,1)}, u32[]{:S(2)}) copy-start(bf16[512,1024]{1,0:T(8,128)(2,1)} %emb_hbm.1) | copy-start | bytes 3145732

commit v3 on v2

--- a/solution.py
+++ b/solution.py
@@ -75,7 +75,7 @@
     loads = [
         pltpu.make_async_copy(src, dst, load_sem.at[k])
         for k, (src, dst) in enumerate(
-            [(assign_hbm, assign), (slot_hbm, slot), (emb_hbm, emb), (counts_hbm, counts)]
+            [(emb_hbm, emb), (assign_hbm, assign), (slot_hbm, slot), (counts_hbm, counts)]
         )
     ]
     for load in loads:
@@ -85,7 +85,7 @@
         pl.semaphore_signal(
             barrier, inc=1, device_id=peer(q), device_id_type=pl.DeviceIdType.MESH
         )
-    for load in loads:
+    for load in loads[1:]:
         load.wait()
 
     flat_slot = (assign[...] ^ me) * cap + slot[...]
@@ -105,6 +105,8 @@
         slots = lax.broadcasted_iota(jnp.int32, (span, rows), 0) + first * cap
         hot = jnp.where(slots == flat_slot, 1.0, 0.0).astype(bf16)
         place[pl.ds(first * cap, span), :] = hot
+        if turn == 0:
+            loads[0].wait()
         block = jnp.dot(hot, emb[...], preferred_element_type=f32).astype(bf16)
         if first == 0:
             members[pl.ds(0, cap), :] = block[:cap]

time: 63.8 us -> 63.8 us (level)
  no operation moved by 1% of the time
where the time goes in v3:
time: 63.8 us; the launch traced here: 63.6 us
  Pallas kernels  59.8 us (94%)
  local copies, waits for them, and re-layouts  3.11 us (5%)
  between operations  0.67 us (1%)
    pallas_call x1, Pallas kernels, fused(): pl.pallas_call(functools.partial(kernel, shards, mirrors, sends), out_sha...  59.8 us
    unnamed x10, local copies, waits for them, and re-layouts  3.11 us

profile of v3, /device:TPU:0, one launch (start us, length us, event | category | flops | bytes accessed | tf_op | source)
XLA Modules:
  0.0 63.6 jit_solution(11664215171171094139)
XLA Ops:
  0.6 0.0 copy-start.2
  0.6 0.0 copy-start.1
  0.7 0.0 copy-start.3
  0.7 0.7 %copy-done.2 = s32[512]{0:T(512)S(1)} copy-done((s32[512]{0:T(512)S(1)}, s32[512]{0:T(512)}, u32[]{:S(2)}) %copy-start.2) | copy-done | bytes 2072
  1.3 0.0 copy-done.1
  1.3 0.0 copy-done.3
  1.3 0.0 copy-start
  1.3 1.2 %copy-done = bf16[512,1024]{1,0:T(8,128)(2,1)S(1)} copy-done((bf16[512,1024]{1,0:T(8,128)(2,1)S(1)}, bf16[512,1024]{1,0:T(8,128)(2,1)}, u32[]{:S(2)}) %copy-start) | copy-done | bytes 1048600
  2.6 59.8 %shard_map.59 = (f32[1,512]{1,0:T(1,128)S(1)}, f32[16,1024]{1,0:T(8,128)S(1)}) custom-call(bf16[512,1024]{1,0:T(8,128)(2,1)S(1)} %copy-done, s32[1,512]{1,0:T(1,128)S(1)} %bitcast.4, s32[1,512]{1,0:T(1,128)S(1)} %bitcast.5, s32[1,16]{1,0:T(1,128)S(1)} %bitcast.7), custom_call_target="tpu_custom_call" | custom-call | tf_op jit(solution)/shard_map/pallas_call | solution.py:220
  62.4 0.6 copy.8
  63.0 0.6 copy.9
Async XLA Ops:
  0.6 0.7 %copy-start.2 = (s32[512]{0:T(512)S(1)}, s32[512]{0:T(512)}, u32[]{:S(2)}) copy-start(s32[512]{0:T(512)} %param.7) | copy-start | bytes 6148
  0.6 0.7 %copy-start.1 = (s32[512]{0:T(512)S(1)}, s32[512]{0:T(512)}, u32[]{:S(2)}) copy-start(s32[512]{0:T(512)} %param.5) | copy-start | bytes 6148
  0.7 0.7 %copy-start.3 = (s32[16]{0:T(128)S(1)}, s32[16]{0:T(128)}, u32[]{:S(2)}) copy-start(s32[16]{0:T(128)} %param.6) | copy-start | bytes 196
  1.3 1.2 %copy-start = (bf16[512,1024]{1,0:T(8,128)(2,1)S(1)}, bf16[512,1024]{1,0:T(8,128)(2,1)}, u32[]{:S(2)}) copy-start(bf16[512,1024]{1,0:T(8,128)(2,1)} %emb_hbm.1) | copy-start | bytes 3145732

commit v4 on v2

--- a/solution.py
+++ b/solution.py
@@ -25,16 +25,12 @@
     shards,
     mirrors,
     sends,
-    emb_hbm,
-    assign_hbm,
-    slot_hbm,
-    counts_hbm,
-    score_ref,
-    cent_ref,
     emb,
     assign,
     slot,
     counts,
+    score_ref,
+    cent_ref,
     place,
     outgoing,
     members,
@@ -42,7 +38,6 @@
     down,
     reply_out,
     reply_in,
-    load_sem,
     row_send,
     row_recv,
     reply_send,
@@ -72,21 +67,11 @@
             device_id_type=pl.DeviceIdType.MESH,
         )
 
-    loads = [
-        pltpu.make_async_copy(src, dst, load_sem.at[k])
-        for k, (src, dst) in enumerate(
-            [(assign_hbm, assign), (slot_hbm, slot), (emb_hbm, emb), (counts_hbm, counts)]
-        )
-    ]
-    for load in loads:
-        load.start()
     barrier = pltpu.get_barrier_semaphore()
     for q in range(1, n):
         pl.semaphore_signal(
             barrier, inc=1, device_id=peer(q), device_id_type=pl.DeviceIdType.MESH
         )
-    for load in loads:
-        load.wait()
 
     flat_slot = (assign[...] ^ me) * cap + slot[...]
     row_copies = {
@@ -212,7 +197,6 @@
     width = n * capacity
     pair = 2 * capacity
     vmem = pl.BlockSpec(memory_space=pltpu.VMEM)
-    anywhere = pl.BlockSpec(memory_space=pl.ANY)
     half = max(1, shards // 2)
     sends = sorted(range(shards), key=lambda dz: (dz % half, -dz))
     scores, centroids = pl.pallas_call(
@@ -221,13 +205,9 @@
             jax.ShapeDtypeStruct((1, rows), f32),
             jax.ShapeDtypeStruct((n, features), f32),
         ),
-        in_specs=[anywhere] * 4,
+        in_specs=[vmem] * 4,
         out_specs=(vmem, vmem),
         scratch_shapes=[
-            pltpu.VMEM((rows, features), bf16),
-            pltpu.VMEM((1, rows), jnp.int32),
-            pltpu.VMEM((1, rows), jnp.int32),
-            pltpu.VMEM((1, n), jnp.int32),
             pltpu.VMEM((width, rows), bf16),
             pltpu.VMEM((width, features), bf16),
             pltpu.VMEM((width, features), bf16),
@@ -235,7 +215,6 @@
             pltpu.VMEM((8, width), f32),
             pltpu.VMEM((n // 2, 1, features + pair), f32),
             pltpu.VMEM((n, 1, features + pair), f32),
-            pltpu.SemaphoreType.DMA((4,)),
         ]
         + [pltpu.SemaphoreType.DMA((n,))] * 4,
         compiler_params=pltpu.CompilerParams(

time: 63.8 us -> 63.6 us (level)
  no operation moved by 1% of the time
where the time goes in v4:
time: 63.6 us; the launch traced here: 63.4 us
  Pallas kernels  59.7 us (94%)
  local copies, waits for them, and re-layouts  3.11 us (5%)
  between operations  0.67 us (1%)
    pallas_call x1, Pallas kernels, fused(): pl.pallas_call(functools.partial(kernel, shards, mirrors, sends), out_sha...  59.7 us
    unnamed x10, local copies, waits for them, and re-layouts  3.11 us

profile of v4, /device:TPU:0, one launch (start us, length us, event | category | flops | bytes accessed | tf_op | source)
XLA Modules:
  0.0 63.4 jit_solution(12818099472724219333)
XLA Ops:
  0.6 0.0 copy-start.2
  0.6 0.0 copy-start.1
  0.7 0.0 copy-start.3
  0.7 0.7 %copy-done.2 = s32[512]{0:T(512)S(1)} copy-done((s32[512]{0:T(512)S(1)}, s32[512]{0:T(512)}, u32[]{:S(2)}) %copy-start.2) | copy-done | bytes 2072
  1.3 0.0 copy-done.1
  1.3 0.0 copy-done.3
  1.3 0.0 copy-start
  1.3 1.2 %copy-done = bf16[512,1024]{1,0:T(8,128)(2,1)S(1)} copy-done((bf16[512,1024]{1,0:T(8,128)(2,1)S(1)}, bf16[512,1024]{1,0:T(8,128)(2,1)}, u32[]{:S(2)}) %copy-start) | copy-done | bytes 1048600
  2.6 59.7 %shard_map.59 = (f32[1,512]{1,0:T(1,128)S(1)}, f32[16,1024]{1,0:T(8,128)S(1)}) custom-call(bf16[512,1024]{1,0:T(8,128)(2,1)S(1)} %copy-done, s32[1,512]{1,0:T(1,128)S(1)} %bitcast.4, s32[1,512]{1,0:T(1,128)S(1)} %bitcast.5, s32[1,16]{1,0:T(1,128)S(1)} %bitcast.7), custom_call_target="tpu_custom_call" | custom-call | tf_op jit(solution)/shard_map/pallas_call | solution.py:202
  62.2 0.6 copy.8
  62.8 0.6 copy.9
Async XLA Ops:
  0.6 0.7 %copy-start.2 = (s32[512]{0:T(512)S(1)}, s32[512]{0:T(512)}, u32[]{:S(2)}) copy-start(s32[512]{0:T(512)} %param.7) | copy-start | bytes 6148
  0.6 0.7 %copy-start.1 = (s32[512]{0:T(512)S(1)}, s32[512]{0:T(512)}, u32[]{:S(2)}) copy-start(s32[512]{0:T(512)} %param.5) | copy-start | bytes 6148
  0.7 0.7 %copy-start.3 = (s32[16]{0:T(128)S(1)}, s32[16]{0:T(128)}, u32[]{:S(2)}) copy-start(s32[16]{0:T(128)} %param.6) | copy-start | bytes 196
  1.3 1.2 %copy-start = (bf16[512,1024]{1,0:T(8,128)(2,1)S(1)}, bf16[512,1024]{1,0:T(8,128)(2,1)}, u32[]{:S(2)}) copy-start(bf16[512,1024]{1,0:T(8,128)(2,1)} %emb.1) | copy-start | bytes 3145732
